TPU v7x, 32 devices: a whole 2x2x4 slice. The times are simulated.
32 devices in a mesh: ctx: 16 (over z, y, core), tp: 2 (over x).
Axes of the slice: x: 2, y: 2, z: 4, core: 2. Of those that a mesh axis runs over, the one named last changes fastest.
Arguments:
- tokens: bfloat16 [6144, 3072], P('ctx', 'tp'), may hold values from -6 to 6
- queries: bfloat16 [6144, 2048], P('ctx', 'tp'), may hold values from -16 to 16
- key_rows: bfloat16 [6144, 2048], P('ctx', 'tp'), may hold values from -16 to 16
- value_rows: bfloat16 [6144, 2048], P('ctx', 'tp'), may hold values from -6 to 6
- clip_ids: int32 [6144], replicated, may hold values from 0 to 3, never falling along the last dimension, each value on 1 to 4608 neighbouring positions
- causal: int32 [4], replicated, may hold values 0 or 1
- modulation: float32 [3, 4, 3072], replicated, may hold values from -3 to 3
- w_mlp: bfloat16 [3072, 6144], P(None, 'tp'), may hold values from -0.109375 to 0.109375
- w_attn_out: bfloat16 [2048, 3072], P('tp'), may hold values from -1 to 1
- w_mlp_out: bfloat16 [6144, 3072], P('tp'), may hold values from -0.078125 to 0.078125
Outputs:
- mixed: float32 [6144, 3072], P(('ctx', 'tp'))
Inputs may be any that keep to these rules, and one draw needn't show every extreme that they name: `clip_ids`: clip numbers never fall along the tokens; each of the 4 clips has 1 to 4608 tokens and one has exactly 4608.
All inputs are finite; a program needn't handle non-finite values.
Results may differ from a plain program's by a relative error of at most 0.0065.
Values may be sent and summed in bfloat16 or wider, within the bound.
No kernel may reach another device: no remote copies, remote signals or barrier semaphores. Data moves between devices by JAX's collectives and lax.ppermute only.
A program may use at most 192 MiB of HBM per device.

v0:
```python
import functools
import math

import jax
import jax.numpy as jnp
from jax import lax
from jax.experimental import pallas as pl
from jax.experimental.pallas import tpu as pltpu
from jax.sharding import PartitionSpec as P

HD = 128
LANES = 128
ONES_ROWS = 8
KEY_WIDTH = 2 * HD
MASKED = -3e38
COST_SCALE = 1
SPLIT_GRANT = 60
MLP_GRANT = 44
PROJECT_GRANT = 50
START_MAX = -1e30
EPS_NORM = 1e-06
EXP2_SCALE = math.log2(math.e) / math.sqrt(HD)

ANY = pl.BlockSpec(memory_space=pl.ANY)
HBM = pl.BlockSpec(memory_space=pltpu.HBM)
SMEM = pl.BlockSpec(memory_space=pltpu.SMEM)
VMEM = pl.BlockSpec(memory_space=pltpu.VMEM)


def params(mebibytes):
    return pltpu.CompilerParams(vmem_limit_bytes=mebibytes << 20)


def cost(flops, nbytes, exps=0):
    return pl.CostEstimate(
        flops=flops // COST_SCALE, bytes_accessed=nbytes // COST_SCALE, transcendentals=exps // COST_SCALE
    )


def met(place, m, other):
    core = lax.bitwise_xor(place[1], other)
    return lax.bitwise_xor(place[0], 2 * m + core)


def token_base(place, m, other, group, rows):
    core = lax.bitwise_xor(lax.bitwise_xor(place[1], other), group)
    return (met(place, m, other) * 2 + core) * rows


def split_kernel(
    ways, chunk_rows, place, q_hbm, k_hbm, v_hbm, keep, give, q, k, v, sems
):
    rows = q.shape[0]
    share = rows // 2
    copies = [
        pltpu.make_async_copy(source, target, sems.at[i])
        for i, (source, target) in enumerate(((k_hbm, k), (v_hbm, v), (q_hbm, q)))
    ]
    for copy in copies:
        copy.start()
    for copy in copies:
        copy.wait()
    for side, out in enumerate((give, keep)):
        for m in range(ways):
            head = met(place, m, 1 - side)
            columns = pl.ds(pl.multiple_of(head * HD, HD), HD)
            out[m, 0] = k[:, columns]
            for at in range(0, rows, LANES):
                block = v[at : at + LANES, columns].astype(jnp.float32)
                out[m, 1, at : at + LANES, :] = jnp.transpose(block).astype(jnp.bfloat16)
            first = 0
            for count in chunk_rows:
                half = count // 2
                start = 2 * first
                out[m, 2, start : start + half] = q[first : first + half, columns]
                out[m, 2, start + half : start + count] = q[
                    share + first : share + first + half, columns
                ]
                first += half


def split_heads(scalars, ways, chunk_rows, queries, key_rows, value_rows):
    rows = queries.shape[0]
    shape = jax.ShapeDtypeStruct((ways, 3, rows, HD), jnp.bfloat16)
    return pl.pallas_call(
        functools.partial(split_kernel, ways, chunk_rows),
        out_shape=[shape, shape],
        in_specs=[SMEM, HBM, HBM, HBM],
        out_specs=[VMEM, VMEM],
        scratch_shapes=[pltpu.VMEM(queries.shape, jnp.bfloat16)] * 3
        + [pltpu.SemaphoreType.DMA((3,))],
        compiler_params=params(SPLIT_GRANT),
        name="split_heads",
    )(scalars, queries, key_rows, value_rows)


def pack_kernel(ways, keep, got, *refs):
    outs, sems = refs[:ways], refs[ways]
    copies = []
    for m in reversed(range(ways)):
        for i, source in enumerate((keep, got)):
            copies.append(
                pltpu.make_async_copy(source.at[m], outs[m].at[:, i], sems.at[2 * m + i])
            )
            copies[-1].start()
    for copy in copies:
        copy.wait()


def pack(keep, got):
    ways, arrays, rows, _ = keep.shape
    return pl.pallas_call(
        functools.partial(pack_kernel, ways),
        out_shape=[jax.ShapeDtypeStruct((arrays, 2, rows, HD), jnp.bfloat16)] * ways,
        in_specs=[ANY, ANY],
        out_specs=[ANY] * ways,
        scratch_shapes=[pltpu.SemaphoreType.DMA((2 * ways,))],
        compiler_params=params(4),
        name="pack",
    )(keep, got)


def pick_kernel(ways, *refs):
    pieces, out, sems = refs[:ways], refs[ways], refs[ways + 1]
    copies = []
    for m in range(ways):
        copies.append(pltpu.make_async_copy(pieces[m].at[1], out.at[m], sems.at[m]))
        copies[-1].start()
    for copy in copies:
        copy.wait()


def pick_others(pieces):
    _, rows, width = pieces[0].shape
    return pl.pallas_call(
        functools.partial(pick_kernel, len(pieces)),
        out_shape=jax.ShapeDtypeStruct((len(pieces), rows, width), jnp.bfloat16),
        in_specs=[ANY] * len(pieces),
        out_specs=ANY,
        scratch_shapes=[pltpu.SemaphoreType.DMA((len(pieces),))],
        compiler_params=params(4),
        name="pick_others",
    )(*pieces)


def clip_lanes(scalars, clips):
    lane = lax.broadcasted_iota(jnp.int32, (1, HD), 1)
    low = jnp.zeros_like(lane)
    high = jnp.zeros_like(lane)
    for clip in range(clips):
        low = jnp.where(lane == clip, scalars[clip], low)
        high = jnp.where(lane == clip, scalars[clip + 1], high)
    return low, high


def assemble_kernel(clips, n_kv, exchanged_pieces, scalars, place, *refs):
    pieces = refs[:n_kv]
    k, v, sems = refs[n_kv:]
    all_keys = k.shape[0]
    copies = []

    def load(source, target):
        copies.append(pltpu.make_async_copy(source, target, sems.at[len(copies)]))
        copies[-1].start()

    for i, piece in enumerate(pieces):
        groups, count = piece.shape[1:3]
        for group in range(groups):
            base = 0
            if exchanged_pieces:
                ways = n_kv // 2
                base = token_base(place, i % ways, i // ways, group, count)
                base = pl.multiple_of(base, LANES)
            load(piece.at[0, group], k.at[pl.ds(base, count), 0:HD])
            for at in range(0, count, LANES):
                columns = pl.ds(pl.multiple_of(base + at, LANES), LANES)
                load(piece.at[1, group, at : at + LANES], v.at[0:HD, columns])
    low, high = clip_lanes(scalars, clips)
    step = math.gcd(all_keys, 768)
    for at in range(0, all_keys, step):
        pos = at + lax.broadcasted_iota(jnp.int32, (step, HD), 0)
        inside = (pos >= low) & (pos < high)
        k[at : at + step, HD:] = jnp.where(inside, 1.0, 0.0).astype(jnp.bfloat16)
    v[HD:, :] = jnp.ones((v.shape[0] - HD, all_keys), jnp.bfloat16)
    for copy in copies:
        copy.wait()


def assemble(clips, scalars, place, kv_pieces, exchanged_pieces):
    all_keys = sum(piece.shape[1] * piece.shape[2] for piece in kv_pieces)
    n_sems = sum(piece.shape[1] * (1 + piece.shape[2] // LANES) for piece in kv_pieces)
    return pl.pallas_call(
        functools.partial(assemble_kernel, clips, len(kv_pieces), exchanged_pieces),
        out_shape=[
            jax.ShapeDtypeStruct((all_keys, KEY_WIDTH), jnp.bfloat16),
            jax.ShapeDtypeStruct((HD + ONES_ROWS, all_keys), jnp.bfloat16),
        ],
        in_specs=[SMEM, SMEM] + [ANY] * len(kv_pieces),
        out_specs=[VMEM, VMEM],
        scratch_shapes=[pltpu.SemaphoreType.DMA((n_sems,))],
        compiler_params=params(16),
        name="assemble",
    )(scalars, place, *kv_pieces)


def span_of(scalars, clips, pos):
    low = jnp.zeros_like(pos)
    high = jnp.zeros_like(pos)
    for clip in range(clips):
        inside = pos >= scalars[clip]
        end = jnp.where(scalars[clips + 1 + clip] != 0, pos + 1, scalars[clip + 1])
        low = jnp.where(inside, scalars[clip], low)
        high = jnp.where(inside, end, high)
    return low, high


def attention_kernel(
    clips, share, start, key_tile, first_way, scalars, place, k, v, *refs
):
    n_query = (len(refs) - 8) // 2
    query_hbm = refs[:n_query]
    out_hbm = refs[n_query : 2 * n_query]
    q, out, total, peak, score_a, score_b, block_peak, sems = refs[2 * n_query :]
    width = q.shape[1]
    groups, rows, _ = out_hbm[0].shape
    half = rows // 2
    none_causal = 1 << 30
    copies = []
    for i in range(n_query):
        arrays = query_hbm[i].shape[0]
        for group in range(groups):
            copies.append(
                pltpu.make_async_copy(
                    query_hbm[i].at[arrays - 1, group, start : start + rows],
                    q.at[i, group * rows : (group + 1) * rows, 0:HD],
                    sems.at[i * groups + group],
                )
            )
            copies[-1].start()
    clip_low, clip_high = clip_lanes(scalars, clips)
    for copy in copies:
        copy.wait()
    scores = [score_a, score_b]
    leaving = [
        [
            pltpu.make_async_copy(
                out.at[i, group * rows : (group + 1) * rows],
                out_hbm[i].at[group],
                sems.at[i * groups + group],
            )
            for group in range(groups)
        ]
        for i in range(n_query)
    ]

    def positions(shape, axis, firsts):
        index = lax.broadcasted_iota(jnp.int32, shape, axis)
        pos = index
        for group, first in enumerate(firsts):
            at = group * rows
            pos = jnp.where(index >= at, index + (first - at), pos)
            pos = jnp.where(index >= at + half, index + (first + share - at - half), pos)
        return pos

    def one_tile(piece, _):
        if first_way is not None:
            firsts = [
                token_base(place, first_way + piece, 0, group, 2 * share) + start // 2
                for group in range(groups)
            ]
        else:
            firsts = [place[0]]
        begin, end, causal_from = none_causal, 0, none_causal
        for first in firsts:
            last = first + share + half - 1
            begin = jnp.minimum(begin, span_of(scalars, clips, first)[0])
            end = jnp.maximum(end, span_of(scalars, clips, last)[1])
            for clip in range(clips):
                met = (first < scalars[clip + 1]) & (last >= scalars[clip])
                met = met & (scalars[clips + 1 + clip] != 0)
                causal_from = jnp.where(
                    met, jnp.minimum(causal_from, jnp.maximum(first, scalars[clip])), causal_from
                )
        begin = begin // key_tile
        end = (end + key_tile - 1) // key_tile
        pos = positions((1, width), 1, firsts)
        last_key = jnp.full_like(pos, none_causal)
        for clip in range(clips):
            inside = (pos >= scalars[clip]) & (pos < scalars[clip + 1])
            inside = inside & (scalars[clips + 1 + clip] != 0)
            last_key = jnp.where(inside, pos, last_key)
        row_pos = positions((width, HD), 0, firsts)
        inside = (row_pos >= clip_low) & (row_pos < clip_high)
        q[piece, :, HD:] = jnp.where(inside, 0.0, MASKED).astype(jnp.bfloat16)
        total[...] = jnp.zeros_like(total)
        peak[...] = jnp.full_like(peak, START_MAX)

        def multiply(tile, slot):
            keys = k[pl.ds(pl.multiple_of(tile * key_tile, key_tile), key_tile), :]
            block = lax.dot_general(
                keys, q[piece], (((1,), (1,)), ((), ())), preferred_element_type=jnp.float32
            )
            scores[slot][...] = block
            block_peak[slot] = jnp.max(block, axis=0, keepdims=True)

        def mask(tile, slot):
            @pl.when((tile + 1) * key_tile - 1 > causal_from)
            def _():
                key_pos = tile * key_tile + lax.broadcasted_iota(jnp.int32, (key_tile, 1), 0)
                block = jnp.where(key_pos <= last_key, scores[slot][...], MASKED)
                scores[slot][...] = block
                block_peak[slot] = jnp.max(block, axis=0, keepdims=True)

        def gather(tile, slot):
            old = peak[...]
            new = jnp.maximum(old, block_peak[slot])
            peak[...] = new
            factor = jnp.exp2((old - new) * EXP2_SCALE)
            weights = jnp.exp2(scores[slot][...] * EXP2_SCALE - new * EXP2_SCALE)
            values = v[:, pl.ds(pl.multiple_of(tile * key_tile, key_tile), key_tile)]
            total[...] = total[...] * factor + jnp.dot(
                values, weights.astype(jnp.bfloat16), preferred_element_type=jnp.float32
            )

        multiply(begin, 0)
        mask(begin, 0)
        count = end - begin

        def two_tiles(pair, _):
            tile = begin + 2 * pair
            multiply(tile + 1, 1)
            gather(tile, 0)
            mask(tile + 1, 1)
            later = jnp.minimum(tile + 2, end - 1)
            multiply(later, 0)
            gather(tile + 1, 1)
            mask(later, 0)
            return 0

        lax.fori_loop(0, count // 2, two_tiles, 0)

        @pl.when(count % 2 == 1)
        def _():
            gather(end - 1, 0)

        both = total[...]
        out[piece] = jnp.transpose(both[:HD] / both[HD : HD + 1]).astype(jnp.bfloat16)
        return 0

    def tile_and_leave(piece, _):
        one_tile(piece, _)
        for i in range(n_query):

            @pl.when(piece == i)
            def _():
                for copy in leaving[i]:
                    copy.start()

        return 0

    lax.fori_loop(0, n_query, tile_and_leave, 0)
    for some in leaving:
        for copy in some:
            copy.wait()


def attention(
    clips, scalars, place, queries, start, rows, k, v, share, first_way, name
):
    n_query = len(queries)
    groups = queries[0].shape[1]
    width = groups * rows
    all_keys = k.shape[0]
    key_tile = math.gcd(all_keys, 768)
    return pl.pallas_call(
        functools.partial(
            attention_kernel, clips, share, start, key_tile, first_way
        ),
        out_shape=[jax.ShapeDtypeStruct((groups, rows, HD), jnp.bfloat16)] * n_query,
        in_specs=[SMEM, SMEM, VMEM, VMEM] + [ANY] * n_query,
        out_specs=[ANY] * n_query,
        scratch_shapes=[
            pltpu.VMEM((n_query, width, KEY_WIDTH), jnp.bfloat16),
            pltpu.VMEM((n_query, width, HD), jnp.bfloat16),
            pltpu.VMEM((HD + ONES_ROWS, width), jnp.float32),
            pltpu.VMEM((1, width), jnp.float32),
            pltpu.VMEM((key_tile, width), jnp.float32),
            pltpu.VMEM((key_tile, width), jnp.float32),
            pltpu.VMEM((2, 1, width), jnp.float32),
            pltpu.SemaphoreType.DMA((n_query * groups,)),
        ],
        compiler_params=params(20),
        cost_estimate=cost(
            4 * n_query * width * all_keys * HD, 4 * all_keys * HD, n_query * width * all_keys
        ),
        name=name,
    )(scalars, place, k, v, *queries)


def value_blocks(values):
    count = values.shape[0]
    return jnp.swapaxes(values.reshape(count // LANES, LANES, HD), 1, 2).reshape(count, HD)


def select_rows(ids, table, clips):
    picked = jnp.broadcast_to(table[0:1], (ids.shape[0], table.shape[1]))
    for clip in range(1, clips):
        picked = jnp.where(ids == clip, table[clip : clip + 1], picked)
    return picked


def mlp_in_kernel(clips, n_parts, place, ids_ref, modulation_ref, *refs):
    parts = refs[:n_parts]
    w_in, hidden, modulated = refs[n_parts:]
    width = modulated.shape[1]

    @pl.when(pl.program_id(0) == 0)
    def _():
        part_width = width // n_parts
        mean = sum(
            jnp.sum(part[...].astype(jnp.float32), axis=1, keepdims=True) for part in parts
        ) / width
        variance = sum(
            jnp.sum((part[...].astype(jnp.float32) - mean) ** 2, axis=1, keepdims=True)
            for part in parts
        ) / width
        inverse = lax.rsqrt(variance + EPS_NORM)
        ids = ids_ref[...]
        for i, part in enumerate(parts):
            part_at = lax.bitwise_xor(place[2], i) if n_parts > 1 else 0
            columns = pl.ds(pl.multiple_of(part_at * part_width, LANES), part_width)
            normed = (part[...].astype(jnp.float32) - mean) * inverse
            shift = select_rows(ids, modulation_ref[0, :, columns], clips)
            scale = select_rows(ids, modulation_ref[1, :, columns], clips)
            modulated[:, columns] = (normed * (1.0 + scale) + shift).astype(jnp.bfloat16)

    hidden[...] = jax.nn.gelu(
        jnp.dot(modulated[...], w_in[...], preferred_element_type=jnp.float32), approximate=True
    ).astype(jnp.bfloat16)


def mlp_in(clips, order, ids, modulation, parts, w_in):
    rows = parts[0].shape[0]
    width, units = w_in.shape
    block = math.gcd(units, 512)
    return pl.pallas_call(
        functools.partial(mlp_in_kernel, clips, len(parts)),
        grid=(units // block,),
        out_shape=jax.ShapeDtypeStruct((rows, units), jnp.bfloat16),
        in_specs=[SMEM, VMEM, VMEM]
        + [VMEM] * len(parts)
        + [pl.BlockSpec((width, block), lambda i: (0, i))],
        out_specs=pl.BlockSpec((rows, block), lambda i: (0, i)),
        scratch_shapes=[pltpu.VMEM((rows, width), jnp.bfloat16)],
        compiler_params=params(MLP_GRANT),
        cost_estimate=cost(2 * rows * width * units, 2 * width * units),
        name="mlp_in",
    )(order, ids[:, None], modulation, *parts, w_in)


def mlp_out_kernel(hidden, w_out, branch):
    branch[...] = jnp.dot(hidden[...], w_out[...], preferred_element_type=jnp.float32)


def mlp_out(hidden, w_out):
    rows, units = hidden.shape
    width = w_out.shape[1]
    block = math.gcd(width, 512)
    return pl.pallas_call(
        mlp_out_kernel,
        grid=(width // block,),
        out_shape=jax.ShapeDtypeStruct((rows, width), jnp.float32),
        in_specs=[VMEM, pl.BlockSpec((units, block), lambda i: (0, i))],
        out_specs=pl.BlockSpec((rows, block), lambda i: (0, i)),
        compiler_params=params(MLP_GRANT),
        cost_estimate=cost(2 * rows * width * units, 2 * width * units + 4 * rows * width),
        name="mlp_out",
    )(hidden, w_out)


def project_kernel(ways, first, side, blocks, place, *refs):
    pieces = 2 * ways
    attended = refs[:ways]
    got, w_hbm, mlp_hbm, out, gathered, w, branch, sems = refs[ways:]
    half, width = out.shape
    share = mlp_hbm.shape[0] // 2
    block = width // blocks
    owner = lax.bitwise_xor(place[2], side)
    start = pl.multiple_of(owner * share + first, math.gcd(share, half))
    rows = pltpu.make_async_copy(mlp_hbm.at[pl.ds(start, half)], branch, sems.at[blocks])
    copies = []
    for i in range(blocks):
        columns = slice(i * block, (i + 1) * block)
        copies.append(pltpu.make_async_copy(w_hbm.at[:, columns], w.at[:, columns], sems.at[i]))
    for copy in [copies[0], rows] + copies[1:]:
        copy.start()
    at = pl.multiple_of(owner * half, half)
    for i in range(pieces):
        head = met(place, i % ways, i // ways)
        columns = pl.ds(pl.multiple_of(head * HD, HD), HD)
        if i < ways:
            gathered[:, columns] = attended[i][0, pl.ds(at, half), :]
        else:
            gathered[:, columns] = got[i - ways, pl.ds(at, half), :]
    for i in range(blocks):
        columns = slice(i * block, (i + 1) * block)
        copies[i].wait()
        product = jnp.dot(gathered[...], w[:, columns], preferred_element_type=jnp.float32)
        if i == 0:
            rows.wait()
        out[:, columns] = (branch[:, columns] + product).astype(out.dtype)


def project(scalars, attended, got, w_attn_out, mlp_branch, first, side, dtype, name):
    width = mlp_branch.shape[1]
    ways, half = len(attended), got.shape[1] // 2
    inputs = w_attn_out.shape[0]
    blocks = width // math.gcd(width, 768)
    return pl.pallas_call(
        functools.partial(project_kernel, ways, first, side, blocks),
        out_shape=jax.ShapeDtypeStruct((half, width), dtype),
        in_specs=[SMEM] + [VMEM] * (ways + 1) + [HBM, HBM],
        out_specs=VMEM,
        scratch_shapes=[
            pltpu.VMEM((half, inputs), jnp.bfloat16),
            pltpu.VMEM((inputs, width), jnp.bfloat16),
            pltpu.VMEM((half, width), jnp.float32),
            pltpu.SemaphoreType.DMA((blocks + 1,)),
        ],
        compiler_params=params(PROJECT_GRANT),
        cost_estimate=cost(1, 1),
        name=name,
    )(scalars, *attended, got, w_attn_out, mlp_branch)


def per_device(
    tokens,
    queries,
    key_rows,
    value_rows,
    clip_ids,
    causal,
    modulation,
    w_mlp,
    w_attn_out,
    w_mlp_out,
):
    local_rows = queries.shape[0]
    heads = queries.shape[1] // HD
    clips = causal.shape[0]
    tp_size = lax.axis_size("tp")
    ctx_size = lax.axis_size("ctx")
    here = lax.axis_index("ctx")
    tp_here = lax.axis_index("tp")
    first_row = here * local_rows
    own_ids = lax.dynamic_slice_in_dim(clip_ids, first_row, local_rows)
    clip_starts = jnp.sum(
        (clip_ids[None, :] < jnp.arange(clips + 1, dtype=jnp.int32)[:, None]).astype(jnp.int32),
        axis=1,
    )
    clip_scalars = jnp.concatenate([clip_starts, causal])
    share = local_rows // tp_size

    chips = ctx_size // 2
    split = (
        tp_size == 2
        and ctx_size % 2 == 0
        and chips & (chips - 1) == 0
        and heads == chips
        and local_rows == 3 * LANES
    )
    if split:
        return exchanged(
            tokens, queries, key_rows, value_rows, own_ids, clip_scalars, clips, modulation,
            w_mlp, w_attn_out, w_mlp_out, chips,
        )

    place = jnp.stack([first_row, 0, tp_here])
    full_rows = lax.all_gather(tokens, "tp", axis=1, tiled=True)
    hidden = mlp_in(clips, place, own_ids, modulation, [full_rows], w_mlp)
    branch = mlp_out(hidden, w_mlp_out)
    all_keys = lax.all_gather(key_rows, "ctx", axis=0, tiled=True)
    all_values = lax.all_gather(value_rows, "ctx", axis=0, tiled=True)
    attended = []
    for head in range(heads):
        columns = slice(head * HD, (head + 1) * HD)
        kv = jnp.stack([all_keys[:, columns], value_blocks(all_values[:, columns])])
        k, v = assemble(clips, clip_scalars, place, [kv[:, None]], False)
        attended.extend(
            attention(
                clips, clip_scalars, place, [queries[None, None, :, columns]], 0, local_rows,
                k, v, local_rows // 2, None, "attention",
            )
        )
    branch = lax.psum_scatter(
        branch
        + jnp.dot(jnp.concatenate([one[0] for one in attended], axis=1), w_attn_out, preferred_element_type=jnp.float32),
        "tp",
        scatter_dimension=0,
        tiled=True,
    )
    residual = lax.dynamic_slice_in_dim(full_rows, tp_here * share, share, 0)
    share_ids = lax.dynamic_slice_in_dim(own_ids, tp_here * share, share)
    gate_rows = select_rows(share_ids[:, None], modulation[2], clips)
    return residual.astype(jnp.float32) + gate_rows * branch


def exchanged(
    tokens, queries, key_rows, value_rows, own_ids, clip_scalars, clips, modulation,
    w_mlp, w_attn_out, w_mlp_out, chips,
):
    local_rows = queries.shape[0]
    share = local_rows // 2
    here = lax.axis_index("ctx")
    tp_here = lax.axis_index("tp")
    ways = chips // 2
    chunk_rows = (2 * LANES, LANES)

    def swap_tp(array):
        return lax.ppermute(array, "tp", [(0, 1), (1, 0)])

    def swap_cores(array):
        pairs = [(2 * i + c, 2 * i + 1 - c) for i in range(chips) for c in (0, 1)]
        return lax.ppermute(array, "ctx", pairs)

    def exchange(array, m):
        pairs = [(2 * i + c, 2 * (i ^ (2 * m + c)) + c) for i in range(chips) for c in (0, 1)]
        return lax.ppermute(array, "ctx", pairs)

    place = jnp.stack([here // 2, here % 2, tp_here])
    other_half = swap_tp(tokens)
    keep, give = split_heads(
        place, ways, chunk_rows, queries, key_rows, value_rows
    )
    messages = pack(keep, swap_cores(give))
    own_pieces = [None] * ways
    for m in reversed(range(ways)):
        own_pieces[m] = exchange(messages[m], m)
    parts = [tokens, other_half]
    hidden = mlp_in(clips, place, own_ids, modulation, parts, w_mlp)
    mlp_branch = mlp_out(hidden, w_mlp_out)
    for m in reversed(range(ways)):
        own_pieces[m], mlp_branch = lax.optimization_barrier((own_pieces[m], mlp_branch))
    core_pieces = [swap_cores(piece) for piece in own_pieces]

    k, v = assemble(clips, clip_scalars, place, own_pieces + core_pieces, True)

    def attend(chunk, some, clip_scalars, name):
        start = sum(chunk_rows[:chunk])
        return attention(
            clips, clip_scalars, place, [own_pieces[m] for m in some], start,
            chunk_rows[chunk], k, v, share, some[0], name,
        )

    def send_back(outs, some):
        return [exchange(piece, m) for m, piece in zip(some, outs)]

    def kept_rows(chunk, attended, got):
        return project(
            place, attended, got, w_attn_out, mlp_branch,
            sum(chunk_rows[:chunk]) // 2, 0, jnp.float32, "project_kept_%d" % chunk,
        )

    def sent_rows(chunk, attended, got):
        return project(
            place, attended, got, w_attn_out, mlp_branch,
            sum(chunk_rows[:chunk]) // 2, 1, jnp.bfloat16, "project_sent_%d" % chunk,
        )

    near, far = range(ways // 2), range(ways // 2, ways)
    first_outs = attend(0, range(ways), clip_scalars, "attention_0")
    first = send_back(first_outs, range(ways))
    clip_scalars, _ = lax.optimization_barrier((clip_scalars, first_outs[0]))
    far_outs = attend(1, far, clip_scalars, "attention_1_far")
    first, far_outs = lax.optimization_barrier((first, far_outs))
    first_got = swap_cores(pick_others(first))
    first_sent = sent_rows(0, first, first_got)
    far_second = send_back(far_outs, far)
    clip_scalars, first_sent = lax.optimization_barrier((clip_scalars, first_sent))
    first_came = swap_tp(first_sent)
    near_outs = attend(1, near, clip_scalars, "attention_1_near")
    far_second, near_outs = lax.optimization_barrier((far_second, near_outs))
    second = send_back(near_outs, near) + far_second
    first, near_outs = lax.optimization_barrier((first, near_outs))
    first_kept = kept_rows(0, first, first_got)
    second, first_kept = lax.optimization_barrier((second, first_kept))
    second_got = swap_cores(pick_others(second))
    second_sent = sent_rows(1, second, second_got)
    second_sent, first_came = lax.optimization_barrier((second_sent, first_came))
    second_came = swap_tp(second_sent)
    tokens, other_half, own_ids, second, second_sent = lax.optimization_barrier(
        (tokens, other_half, own_ids, second, second_sent)
    )
    second_kept = kept_rows(1, second, second_got)
    own = [
        lax.dynamic_slice_in_dim(part, tp_here * share, share, 0) for part in (tokens, other_half)
    ]
    residual = jnp.where(
        tp_here == 0, jnp.concatenate(own, axis=1), jnp.concatenate(own[::-1], axis=1)
    ).astype(jnp.float32)
    share_ids = lax.dynamic_slice_in_dim(own_ids, tp_here * share, share)
    gate_rows = select_rows(share_ids[:, None], modulation[2], clips)
    cut = first_kept.shape[0]
    begun = residual[:cut] + gate_rows[:cut] * (first_kept + first_came.astype(jnp.float32))
    rest = residual[cut:] + gate_rows[cut:] * second_kept
    begun, rest, gate_rest = lax.optimization_barrier((begun, rest, gate_rows[cut:]))
    rest = rest + gate_rest * second_came.astype(jnp.float32)
    return jnp.concatenate([begun, rest], axis=0)


def solution(mesh):
    in_specs = (
        P("ctx", "tp"),
        P("ctx", "tp"),
        P("ctx", "tp"),
        P("ctx", "tp"),
        P(),
        P(),
        P(),
        P(None, "tp"),
        P("tp", None),
        P("tp", None),
    )
    out_specs = P(("ctx", "tp"), None)
    return jax.shard_map(
        per_device, mesh=mesh, in_specs=in_specs, out_specs=out_specs, check_vma=False
    )
```

profile of v0, /device:TPU:0, one launch (start us, length us, event | category | flops | bytes accessed | tf_op | source)
XLA Modules:
  0.0 146.6 jit_solution(4393404715967442606)
XLA Ops:
  0.6 4.3 %split_heads.1 = (bf16[4,3,384,128]{3,2,1,0:T(8,128)(2,1)}, bf16[4,3,384,128]{3,2,1,0:T(8,128)(2,1)}) custom-call(s32[3]{0:T(128)} %pad_add_fusion.1.place, bf16[384,1024]{1,0:T(8,128)(2,1)} %q_hbm.1, bf16[384,1024]{1,0:T(8,128)(2,1)} %k_hbm.1, bf16[384,1024]{1,0:T(8,128)(2,1)} %v_hbm.1), custom_call_target="tpu_custom_call" | custom-call | tf_op jit(solution)/shard_map/split_heads/pallas_call | solution.py:85
  5.4 2.6 %collective-permute-start = (bf16[384,1536]{1,0:T(8,128)(2,1)S(1)}, bf16[384,1536]{1,0:T(8,128)(2,1)S(1)}, u32[]{:S(2)}, u32[]{:S(2)}) collective-permute-start(bf16[384,1536]{1,0:T(8,128)(2,1)S(1)} %copy-done.2), channel_id=1, source_target_pairs={{0,1},{1,0},{2,3},{3,2},{4,5},{5,4},{6,7},{7,6},{8,9},{9,8},{10,11... | collective-permute-start | bytes 3538952 | tf_op jit(solution)/shard_map/ppermute | solution.py:620
  10.4 4.2 %collective-permute-start.5 = (bf16[3,2,384,128]{3,2,1,0:T(8,128)(2,1)S(1)}, bf16[3,2,384,128]{3,2,1,0:T(8,128)(2,1)S(1)}, u32[]{:S(2)}, u32[]{:S(2)}) collective-permute-start(bf16[3,2,384,128]{3,2,1,0:T(8,128)(2,1)S(1)} %get-tuple-element.68), channel_id=1, source_target_pairs={{0,24},{2,30},{4,28},{6,26},{8,16},{10,22},{12,20},{14,18},{16,8},... | collective-permute-start | bytes 1769480 | tf_op jit(solution)/shard_map/ppermute | solution.py:628
  16.0 18.5 %collective-permute-done.refs_1_ = bf16[384,1536]{1,0:T(8,128)(2,1)S(1)} collective-permute-done((bf16[384,1536]{1,0:T(8,128)(2,1)S(1)}, bf16[384,1536]{1,0:T(8,128)(2,1)S(1)}, u32[]{:S(2)}, u32[]{:S(2)}) %collective-permute-start) | collective-permute-done | bytes 1179680 | tf_op jit(solution)/shard_map/ppermute | solution.py:620
  34.5 16.9 %mlp_in.1.hidden = bf16[384,3072]{1,0:T(8,128)(2,1)S(1)} custom-call(s32[3]{0:T(128)S(1)} %copy-done.6, s32[384,1]{1,0:T(8,128)S(1)} %broadcast_in_dim.67.ids_ref, f32[3,4,3072]{2,1,0:T(4,128)S(1)} %copy-done.7, bf16[384,1536]{1,0:T(8,128)(2,1)S(1)} %copy-done.2, bf16[384,1536]{1,0:T(8,128)(2,1)S(1)} %collective-permute-done.refs_1_, bf16[3072,3072]{1,0:T(8,128)(2,1)} %refs_2_.1), custom_call_target="tpu_custom_call" | custom-call | flops 7247757312 | bytes 18874368 | tf_op jit(solution)/shard_map/mlp_in/pallas_call | solution.py:446
  51.5 11.8 %mlp_out.1.refs_6_ = f32[384,3072]{1,0:T(8,128)S(1)} custom-call(bf16[384,3072]{1,0:T(8,128)(2,1)S(1)} %mlp_in.1.hidden, bf16[3072,3072]{1,0:T(8,128)(2,1)} %w_out.1), custom_call_target="tpu_custom_call" | custom-call | flops 7247757312 | bytes 23592960 | tf_op jit(solution)/shard_map/mlp_out/pallas_call | solution.py:469
  63.3 2.7 %collective-permute-done.4.refs_2_.refs_0_ = bf16[3,2,384,128]{3,2,1,0:T(8,128)(2,1)S(1)} collective-permute-done((bf16[3,2,384,128]{3,2,1,0:T(8,128)(2,1)S(1)}, bf16[3,2,384,128]{3,2,1,0:T(8,128)(2,1)S(1)}, u32[]{:S(2)}, u32[]{:S(2)}) %collective-permute-start.4) | collective-permute-done | bytes 589856 | tf_op jit(solution)/shard_map/ppermute | solution.py:628
  70.6 2.6 %assemble.1 = (bf16[6144,256]{1,0:T(8,128)(2,1)S(1)}, bf16[136,6144]{1,0:T(8,128)(2,1)S(1)}) custom-call(s32[9]{0:T(128)S(1)} %pad_add_fusion.scalars, s32[3]{0:T(128)S(1)} %copy-done.6, bf16[3,2,384,128]{3,2,1,0:T(8,128)(2,1)S(1)} %collective-permute-done.2.refs_0_, bf16[3,2,384,128]{3,2,1,0:T(8,128)(2,1)S(1)} %collective-permute-done.3.refs_1_, ...), custom_call_target="tpu_custom_call" | custom-call | tf_op jit(solution)/shard_map/assemble/pallas_call | solution.py:192
  73.3 15.7 %attention_0.1 = (bf16[2,256,128]{2,1,0:T(8,128)(2,1)S(1)}, bf16[2,256,128]{2,1,0:T(8,128)(2,1)S(1)}, bf16[2,256,128]{2,1,0:T(8,128)(2,1)S(1)}, bf16[2,256,128]{2,1,0:T(8,128)(2,1)S(1)}) custom-call(s32[9]{0:T(128)S(1)} %pad_add_fusion.scalars, s32[3]{0:T(128)S(1)} %copy-done.6, bf16[6144,256]{1,0:T(8,128)(2,1)S(1)} %get-tuple-element.76.k, ...), custom_call_target="tpu_custom_call" | custom-call | flops 6442450944 | bytes 3145728 | tf_op jit(solution)/shard_map/attention_0/pallas_call | solution.py:375
  89.9 3.0 %collective-permute-start.12 = (bf16[2,256,128]{2,1,0:T(8,128)(2,1)S(1)}, bf16[2,256,128]{2,1,0:T(8,128)(2,1)S(1)}, u32[]{:S(2)}, u32[]{:S(2)}) collective-permute-start(bf16[2,256,128]{2,1,0:T(8,128)(2,1)S(1)} %get-tuple-element.80), channel_id=1, source_target_pairs={{0,16},{2,22},{4,20},{6,18},{8,24},{10,30},{12,28},{14,26},{16,0},... | collective-permute-start | bytes 393224 | tf_op jit(solution)/shard_map/ppermute | solution.py:628
  94.2 6.7 %attention_1_far.1 = (bf16[2,128,128]{2,1,0:T(8,128)(2,1)S(1)}, bf16[2,128,128]{2,1,0:T(8,128)(2,1)S(1)}) custom-call(s32[9]{0:T(128)S(1)} %pad_add_fusion.scalars, s32[3]{0:T(128)S(1)} %copy-done.6, bf16[6144,256]{1,0:T(8,128)(2,1)S(1)} %get-tuple-element.76.k, bf16[136,6144]{1,0:T(8,128)(2,1)S(1)} %get-tuple-element.77.v, ...), custom_call_target="tpu_custom_call" | custom-call | flops 1610612736 | bytes 3145728 | tf_op jit(solution)/shard_map/attention_1_far/pallas_call | solution.py:375
  101.8 3.6 %collective-permute-start.16 = (bf16[4,256,128]{2,1,0:T(8,128)(2,1)S(1)}, bf16[4,256,128]{2,1,0:T(8,128)(2,1)S(1)}, u32[]{:S(2)}, u32[]{:S(2)}) collective-permute-start(bf16[4,256,128]{2,1,0:T(8,128)(2,1)S(1)} %pick_others.2), channel_id=1, source_target_pairs={{0,2},{2,0},{4,6},{6,4},{8,10},{10,8},{12,14},{14,12},{16,18},{18,... | collective-permute-start | bytes 786440 | tf_op jit(solution)/shard_map/ppermute | solution.py:624
  105.4 2.9 %collective-permute-start.14 = (bf16[2,128,128]{2,1,0:T(8,128)(2,1)S(1)}, bf16[2,128,128]{2,1,0:T(8,128)(2,1)S(1)}, u32[]{:S(2)}, u32[]{:S(2)}) collective-permute-start(bf16[2,128,128]{2,1,0:T(8,128)(2,1)S(1)} %get-tuple-element.85), channel_id=1, source_target_pairs={{0,16},{2,22},{4,20},{6,18},{8,24},{10,30},{12,28},{14,26},{16,0},... | collective-permute-start | bytes 196616 | tf_op jit(solution)/shard_map/ppermute | solution.py:628
  109.7 4.4 %project_sent_0.1 = bf16[128,3072]{1,0:T(8,128)(2,1)S(1)} custom-call(s32[3]{0:T(128)S(1)} %copy-done.6, bf16[2,256,128]{2,1,0:T(8,128)(2,1)S(1)} %collective-permute-done.10.refs_0_, bf16[2,256,128]{2,1,0:T(8,128)(2,1)S(1)} %collective-permute-done.11.refs_1_, bf16[2,256,128]{2,1,0:T(8,128)(2,1)S(1)} %collective-permute-done.12.refs_2_, ...), custom_call_target="tpu_custom_call" | custom-call | flops 1 | bytes 1 | tf_op jit(solution)/shard_map/project_sent_0/pallas_call | solution.py:519
  114.1 1.6 %collective-permute-start.20 = (bf16[128,3072]{1,0:T(8,128)(2,1)S(1)}, bf16[128,3072]{1,0:T(8,128)(2,1)}, u32[]{:S(2)}, u32[]{:S(2)}) collective-permute-start(bf16[128,3072]{1,0:T(8,128)(2,1)S(1)} %project_sent_0.1), channel_id=1, source_target_pairs={{0,1},{1,0},{2,3},{3,2},{4,5},{5,4},{6,7},{7,6},{8,9},{9,8},{10,11... | collective-permute-start | bytes 2359304 | tf_op jit(solution)/shard_map/ppermute | solution.py:620
  115.6 5.0 %attention_1_near.1 = (bf16[2,128,128]{2,1,0:T(8,128)(2,1)S(1)}, bf16[2,128,128]{2,1,0:T(8,128)(2,1)S(1)}) custom-call(s32[9]{0:T(128)S(1)} %pad_add_fusion.scalars, s32[3]{0:T(128)S(1)} %copy-done.6, bf16[6144,256]{1,0:T(8,128)(2,1)S(1)} %get-tuple-element.76.k, bf16[136,6144]{1,0:T(8,128)(2,1)S(1)} %get-tuple-element.77.v, ...), custom_call_target="tpu_custom_call" | custom-call | flops 1610612736 | bytes 3145728 | tf_op jit(solution)/shard_map/attention_1_near/pallas_call | solution.py:375
  121.5 4.4 %project_kept_0.1 = f32[128,3072]{1,0:T(8,128)S(1)} custom-call(s32[3]{0:T(128)S(1)} %copy-done.6, bf16[2,256,128]{2,1,0:T(8,128)(2,1)S(1)} %collective-permute-done.10.refs_0_, bf16[2,256,128]{2,1,0:T(8,128)(2,1)S(1)} %collective-permute-done.11.refs_1_, bf16[2,256,128]{2,1,0:T(8,128)(2,1)S(1)} %collective-permute-done.12.refs_2_, ...), custom_call_target="tpu_custom_call" | custom-call | flops 1 | bytes 1 | tf_op jit(solution)/shard_map/project_kept_0/pallas_call | solution.py:519
  126.1 1.8 %collective-permute-start.19 = (bf16[4,128,128]{2,1,0:T(8,128)(2,1)S(1)}, bf16[4,128,128]{2,1,0:T(8,128)(2,1)S(1)}, u32[]{:S(2)}, u32[]{:S(2)}) collective-permute-start(bf16[4,128,128]{2,1,0:T(8,128)(2,1)S(1)} %pick_others.3), channel_id=1, source_target_pairs={{0,2},{2,0},{4,6},{6,4},{8,10},{10,8},{12,14},{14,12},{16,18},{18,... | collective-permute-start | bytes 393224 | tf_op jit(solution)/shard_map/ppermute | solution.py:624
  128.8 4.1 %project_sent_1.1 = bf16[64,3072]{1,0:T(8,128)(2,1)S(1)} custom-call(s32[3]{0:T(128)S(1)} %copy-done.6, bf16[2,128,128]{2,1,0:T(8,128)(2,1)S(1)} %collective-permute-done.17.refs_0_, bf16[2,128,128]{2,1,0:T(8,128)(2,1)S(1)} %collective-permute-done.18.refs_1_, bf16[2,128,128]{2,1,0:T(8,128)(2,1)S(1)} %collective-permute-done.14.refs_2_, ...), custom_call_target="tpu_custom_call" | custom-call | flops 1 | bytes 1 | tf_op jit(solution)/shard_map/project_sent_1/pallas_call | solution.py:519
  134.1 1.5 %collective-permute-start.21 = (bf16[64,3072]{1,0:T(8,128)(2,1)S(1)}, bf16[64,3072]{1,0:T(8,128)(2,1)S(1)}, u32[]{:S(2)}, u32[]{:S(2)}) collective-permute-start(bf16[64,3072]{1,0:T(8,128)(2,1)S(1)} %project_sent_1.1), channel_id=1, source_target_pairs={{0,1},{1,0},{2,3},{3,2},{4,5},{5,4},{6,7},{7,6},{8,9},{9,8},{10,11... | collective-permute-start | bytes 1179656 | tf_op jit(solution)/shard_map/ppermute | solution.py:620
  136.8 1.5 %fusion = f32[128,3072]{1,0:T(8,128)S(1)} fusion(f32[192,3072]{1,0:T(8,128)S(1)} %select_select_fusion, f32[192,3072]{1,0:T(8,128)S(1)} %fusion.1, f32[128,3072]{1,0:T(8,128)S(1)} %project_kept_0.1, bf16[128,3072]{1,0:T(8,128)(2,1)} %collective-permute-done.20), kind=kLoop, calls=%fused_computation.3 | loop fusion | flops 1572864 | bytes 7077888 | tf_op jit(solution)/shard_map/add | solution.py:704
  138.4 4.1 %project_kept_1.1 = f32[64,3072]{1,0:T(8,128)S(1)} custom-call(s32[3]{0:T(128)S(1)} %copy-done.6, bf16[2,128,128]{2,1,0:T(8,128)(2,1)S(1)} %collective-permute-done.17.refs_0_, bf16[2,128,128]{2,1,0:T(8,128)(2,1)S(1)} %collective-permute-done.18.refs_1_, bf16[2,128,128]{2,1,0:T(8,128)(2,1)S(1)} %collective-permute-done.14.refs_2_, ...), custom_call_target="tpu_custom_call" | custom-call | flops 1 | bytes 1 | tf_op jit(solution)/shard_map/project_kept_1/pallas_call | solution.py:519
  142.6 2.1 %collective-permute-done.21 = bf16[64,3072]{1,0:T(8,128)(2,1)S(1)} collective-permute-done((bf16[64,3072]{1,0:T(8,128)(2,1)S(1)}, bf16[64,3072]{1,0:T(8,128)(2,1)S(1)}, u32[]{:S(2)}, u32[]{:S(2)}) %collective-permute-start.21) | collective-permute-done | bytes 393248 | tf_op jit(solution)/shard_map/ppermute | solution.py:620
  144.9 1.6 %pad_maximum_fusion = f32[192,3072]{1,0:T(8,128)} fusion(f32[64,3072]{1,0:T(8,128)S(1)} %multiply_add_fusion, f32[128,3072]{1,0:T(8,128)S(1)} %fusion), kind=kLoop, calls=%fused_computation | loop fusion | flops 589824 | bytes 4718592 | tf_op jit(solution)/shard_map/concatenate | solution.py:708
  (68 shorter events, 18.5 us)
Async XLA Ops:
  0.6 33.9 %copy-start.6 = (s32[3]{0:T(128)S(1)}, s32[3]{0:T(128)}, u32[]{:S(2)}) copy-start(s32[3]{0:T(128)} %pad_add_fusion.1.place) | copy-start | bytes 40
  4.9 4.0 %collective-permute-start.1 = (bf16[4,3,384,128]{3,2,1,0:T(8,128)(2,1)}, bf16[4,3,384,128]{3,2,1,0:T(8,128)(2,1)S(1)}, u32[]{:S(2)}, u32[]{:S(2)}) collective-permute-start(bf16[4,3,384,128]{3,2,1,0:T(8,128)(2,1)} %get-tuple-element.64), channel_id=1, source_target_pairs={{0,2},{2,0},{4,6},{6,4},{8,10},{10,8},{12,14},{14,12},{16,18},{18,... | collective-permute-start | bytes 3538952 | tf_op jit(solution)/shard_map/ppermute | solution.py:624
  5.4 29.1 %collective-permute-start = (bf16[384,1536]{1,0:T(8,128)(2,1)S(1)}, bf16[384,1536]{1,0:T(8,128)(2,1)S(1)}, u32[]{:S(2)}, u32[]{:S(2)}) collective-permute-start(bf16[384,1536]{1,0:T(8,128)(2,1)S(1)} %copy-done.2), channel_id=1, source_target_pairs={{0,1},{1,0},{2,3},{3,2},{4,5},{5,4},{6,7},{7,6},{8,9},{9,8},{10,11... | collective-permute-start | bytes 3538952 | tf_op jit(solution)/shard_map/ppermute | solution.py:620
  8.0 26.6 %copy-start.7 = (f32[3,4,3072]{2,1,0:T(4,128)S(1)}, f32[3,4,3072]{2,1,0:T(4,128)}, u32[]{:S(2)}) copy-start(f32[3,4,3072]{2,1,0:T(4,128)} %modulation_ref.1) | copy-start | bytes 442372
  10.4 52.9 %collective-permute-start.5 = (bf16[3,2,384,128]{3,2,1,0:T(8,128)(2,1)S(1)}, bf16[3,2,384,128]{3,2,1,0:T(8,128)(2,1)S(1)}, u32[]{:S(2)}, u32[]{:S(2)}) collective-permute-start(bf16[3,2,384,128]{3,2,1,0:T(8,128)(2,1)S(1)} %get-tuple-element.68), channel_id=1, source_target_pairs={{0,24},{2,30},{4,28},{6,26},{8,16},{10,22},{12,20},{14,18},{16,8},... | collective-permute-start | bytes 1769480 | tf_op jit(solution)/shard_map/ppermute | solution.py:628
  14.6 51.4 %collective-permute-start.4 = (bf16[3,2,384,128]{3,2,1,0:T(8,128)(2,1)S(1)}, bf16[3,2,384,128]{3,2,1,0:T(8,128)(2,1)S(1)}, u32[]{:S(2)}, u32[]{:S(2)}) collective-permute-start(bf16[3,2,384,128]{3,2,1,0:T(8,128)(2,1)S(1)} %get-tuple-element.67), channel_id=1, source_target_pairs={{0,16},{2,22},{4,20},{6,18},{8,24},{10,30},{12,28},{14,26},{16,0},... | collective-permute-start | bytes 1769480 | tf_op jit(solution)/shard_map/ppermute | solution.py:628
  14.6 51.4 %collective-permute-start.3 = (bf16[3,2,384,128]{3,2,1,0:T(8,128)(2,1)S(1)}, bf16[3,2,384,128]{3,2,1,0:T(8,128)(2,1)S(1)}, u32[]{:S(2)}, u32[]{:S(2)}) collective-permute-start(bf16[3,2,384,128]{3,2,1,0:T(8,128)(2,1)S(1)} %get-tuple-element.66), channel_id=1, source_target_pairs={{0,8},{2,14},{4,12},{6,10},{8,0},{10,6},{12,4},{14,2},{16,24},{18,... | collective-permute-start | bytes 1769480 | tf_op jit(solution)/shard_map/ppermute | solution.py:628
  15.3 50.8 %collective-permute-start.2 = (bf16[3,2,384,128]{3,2,1,0:T(8,128)(2,1)S(1)}, bf16[3,2,384,128]{3,2,1,0:T(8,128)(2,1)S(1)}, u32[]{:S(2)}, u32[]{:S(2)}) collective-permute-start(bf16[3,2,384,128]{3,2,1,0:T(8,128)(2,1)S(1)} %get-tuple-element.65), channel_id=1, source_target_pairs={{0,0},{2,6},{4,4},{6,2},{8,8},{10,14},{12,12},{14,10},{16,16},{18,... | collective-permute-start | bytes 1769480 | tf_op jit(solution)/shard_map/ppermute | solution.py:628
  66.1 2.0 %collective-permute-start.6 = (bf16[3,2,384,128]{3,2,1,0:T(8,128)(2,1)S(1)}, bf16[3,2,384,128]{3,2,1,0:T(8,128)(2,1)S(1)}, u32[]{:S(2)}, u32[]{:S(2)}) collective-permute-start(bf16[3,2,384,128]{3,2,1,0:T(8,128)(2,1)S(1)} %collective-permute-done.2.refs_0_), channel_id=1, source_target_pairs={{0,2},{2,0},{4,6},{6,4},{8,10},{10,8},{12,14},{14,12},{16,18},{18,... | collective-permute-start | bytes 1769480 | tf_op jit(solution)/shard_map/ppermute | solution.py:624
  66.1 2.8 %collective-permute-start.7 = (bf16[3,2,384,128]{3,2,1,0:T(8,128)(2,1)S(1)}, bf16[3,2,384,128]{3,2,1,0:T(8,128)(2,1)S(1)}, u32[]{:S(2)}, u32[]{:S(2)}) collective-permute-start(bf16[3,2,384,128]{3,2,1,0:T(8,128)(2,1)S(1)} %collective-permute-done.3.refs_1_), channel_id=1, source_target_pairs={{0,2},{2,0},{4,6},{6,4},{8,10},{10,8},{12,14},{14,12},{16,18},{18,... | collective-permute-start | bytes 1769480 | tf_op jit(solution)/shard_map/ppermute | solution.py:624
  66.6 3.2 %collective-permute-start.8 = (bf16[3,2,384,128]{3,2,1,0:T(8,128)(2,1)S(1)}, bf16[3,2,384,128]{3,2,1,0:T(8,128)(2,1)S(1)}, u32[]{:S(2)}, u32[]{:S(2)}) collective-permute-start(bf16[3,2,384,128]{3,2,1,0:T(8,128)(2,1)S(1)} %collective-permute-done.4.refs_2_.refs_0_), channel_id=1, source_target_pairs={{0,2},{2,0},{4,6},{6,4},{8,10},{10,8},{12,14},{14,12},{16,18},{18,... | collective-permute-start | bytes 1769480 | tf_op jit(solution)/shard_map/ppermute | solution.py:624
  66.6 4.0 %collective-permute-start.9 = (bf16[3,2,384,128]{3,2,1,0:T(8,128)(2,1)S(1)}, bf16[3,2,384,128]{3,2,1,0:T(8,128)(2,1)S(1)}, u32[]{:S(2)}, u32[]{:S(2)}) collective-permute-start(bf16[3,2,384,128]{3,2,1,0:T(8,128)(2,1)S(1)} %collective-permute-done.5.refs_3_.refs_1_), channel_id=1, source_target_pairs={{0,2},{2,0},{4,6},{6,4},{8,10},{10,8},{12,14},{14,12},{16,18},{18,... | collective-permute-start | bytes 1769480 | tf_op jit(solution)/shard_map/ppermute | solution.py:624
  88.9 12.0 %collective-permute-start.10 = (bf16[2,256,128]{2,1,0:T(8,128)(2,1)S(1)}, bf16[2,256,128]{2,1,0:T(8,128)(2,1)S(1)}, u32[]{:S(2)}, u32[]{:S(2)}) collective-permute-start(bf16[2,256,128]{2,1,0:T(8,128)(2,1)S(1)} %get-tuple-element.78), channel_id=1, source_target_pairs={{0,0},{2,6},{4,4},{6,2},{8,8},{10,14},{12,12},{14,10},{16,16},{18,... | collective-permute-start | bytes 393224 | tf_op jit(solution)/shard_map/ppermute | solution.py:628
  89.8 11.1 %collective-permute-start.11 = (bf16[2,256,128]{2,1,0:T(8,128)(2,1)S(1)}, bf16[2,256,128]{2,1,0:T(8,128)(2,1)S(1)}, u32[]{:S(2)}, u32[]{:S(2)}) collective-permute-start(bf16[2,256,128]{2,1,0:T(8,128)(2,1)S(1)} %get-tuple-element.79), channel_id=1, source_target_pairs={{0,8},{2,14},{4,12},{6,10},{8,0},{10,6},{12,4},{14,2},{16,24},{18,... | collective-permute-start | bytes 393224 | tf_op jit(solution)/shard_map/ppermute | solution.py:628
  89.9 11.1 %collective-permute-start.12 = (bf16[2,256,128]{2,1,0:T(8,128)(2,1)S(1)}, bf16[2,256,128]{2,1,0:T(8,128)(2,1)S(1)}, u32[]{:S(2)}, u32[]{:S(2)}) collective-permute-start(bf16[2,256,128]{2,1,0:T(8,128)(2,1)S(1)} %get-tuple-element.80), channel_id=1, source_target_pairs={{0,16},{2,22},{4,20},{6,18},{8,24},{10,30},{12,28},{14,26},{16,0},... | collective-permute-start | bytes 393224 | tf_op jit(solution)/shard_map/ppermute | solution.py:628
  92.9 8.6 %collective-permute-start.13 = (bf16[2,256,128]{2,1,0:T(8,128)(2,1)S(1)}, bf16[2,256,128]{2,1,0:T(8,128)(2,1)S(1)}, u32[]{:S(2)}, u32[]{:S(2)}) collective-permute-start(bf16[2,256,128]{2,1,0:T(8,128)(2,1)S(1)} %get-tuple-element.81), channel_id=1, source_target_pairs={{0,24},{2,30},{4,28},{6,26},{8,16},{10,22},{12,20},{14,18},{16,8},... | collective-permute-start | bytes 393224 | tf_op jit(solution)/shard_map/ppermute | solution.py:628
  101.8 7.9 %collective-permute-start.16 = (bf16[4,256,128]{2,1,0:T(8,128)(2,1)S(1)}, bf16[4,256,128]{2,1,0:T(8,128)(2,1)S(1)}, u32[]{:S(2)}, u32[]{:S(2)}) collective-permute-start(bf16[4,256,128]{2,1,0:T(8,128)(2,1)S(1)} %pick_others.2), channel_id=1, source_target_pairs={{0,2},{2,0},{4,6},{6,4},{8,10},{10,8},{12,14},{14,12},{16,18},{18,... | collective-permute-start | bytes 786440 | tf_op jit(solution)/shard_map/ppermute | solution.py:624
  105.4 15.3 %collective-permute-start.14 = (bf16[2,128,128]{2,1,0:T(8,128)(2,1)S(1)}, bf16[2,128,128]{2,1,0:T(8,128)(2,1)S(1)}, u32[]{:S(2)}, u32[]{:S(2)}) collective-permute-start(bf16[2,128,128]{2,1,0:T(8,128)(2,1)S(1)} %get-tuple-element.85), channel_id=1, source_target_pairs={{0,16},{2,22},{4,20},{6,18},{8,24},{10,30},{12,28},{14,26},{16,0},... | collective-permute-start | bytes 196616 | tf_op jit(solution)/shard_map/ppermute | solution.py:628
  108.3 12.4 %collective-permute-start.15 = (bf16[2,128,128]{2,1,0:T(8,128)(2,1)S(1)}, bf16[2,128,128]{2,1,0:T(8,128)(2,1)S(1)}, u32[]{:S(2)}, u32[]{:S(2)}) collective-permute-start(bf16[2,128,128]{2,1,0:T(8,128)(2,1)S(1)} %get-tuple-element.86), channel_id=1, source_target_pairs={{0,24},{2,30},{4,28},{6,26},{8,16},{10,22},{12,20},{14,18},{16,8},... | collective-permute-start | bytes 196616 | tf_op jit(solution)/shard_map/ppermute | solution.py:628
  114.1 20.0 %collective-permute-start.20 = (bf16[128,3072]{1,0:T(8,128)(2,1)S(1)}, bf16[128,3072]{1,0:T(8,128)(2,1)}, u32[]{:S(2)}, u32[]{:S(2)}) collective-permute-start(bf16[128,3072]{1,0:T(8,128)(2,1)S(1)} %project_sent_0.1), channel_id=1, source_target_pairs={{0,1},{1,0},{2,3},{3,2},{4,5},{5,4},{6,7},{7,6},{8,9},{9,8},{10,11... | collective-permute-start | bytes 2359304 | tf_op jit(solution)/shard_map/ppermute | solution.py:620
  120.7 5.1 %collective-permute-start.17 = (bf16[2,128,128]{2,1,0:T(8,128)(2,1)S(1)}, bf16[2,128,128]{2,1,0:T(8,128)(2,1)S(1)}, u32[]{:S(2)}, u32[]{:S(2)}) collective-permute-start(bf16[2,128,128]{2,1,0:T(8,128)(2,1)S(1)} %get-tuple-element.95), channel_id=1, source_target_pairs={{0,0},{2,6},{4,4},{6,2},{8,8},{10,14},{12,12},{14,10},{16,16},{18,... | collective-permute-start | bytes 196616 | tf_op jit(solution)/shard_map/ppermute | solution.py:628
  121.4 4.5 %collective-permute-start.18 = (bf16[2,128,128]{2,1,0:T(8,128)(2,1)S(1)}, bf16[2,128,128]{2,1,0:T(8,128)(2,1)S(1)}, u32[]{:S(2)}, u32[]{:S(2)}) collective-permute-start(bf16[2,128,128]{2,1,0:T(8,128)(2,1)S(1)} %get-tuple-element.96), channel_id=1, source_target_pairs={{0,8},{2,14},{4,12},{6,10},{8,0},{10,6},{12,4},{14,2},{16,24},{18,... | collective-permute-start | bytes 196616 | tf_op jit(solution)/shard_map/ppermute | solution.py:628
  126.1 2.8 %collective-permute-start.19 = (bf16[4,128,128]{2,1,0:T(8,128)(2,1)S(1)}, bf16[4,128,128]{2,1,0:T(8,128)(2,1)S(1)}, u32[]{:S(2)}, u32[]{:S(2)}) collective-permute-start(bf16[4,128,128]{2,1,0:T(8,128)(2,1)S(1)} %pick_others.3), channel_id=1, source_target_pairs={{0,2},{2,0},{4,6},{6,4},{8,10},{10,8},{12,14},{14,12},{16,18},{18,... | collective-permute-start | bytes 393224 | tf_op jit(solution)/shard_map/ppermute | solution.py:624
  134.1 10.7 %collective-permute-start.21 = (bf16[64,3072]{1,0:T(8,128)(2,1)S(1)}, bf16[64,3072]{1,0:T(8,128)(2,1)S(1)}, u32[]{:S(2)}, u32[]{:S(2)}) collective-permute-start(bf16[64,3072]{1,0:T(8,128)(2,1)S(1)} %project_sent_1.1), channel_id=1, source_target_pairs={{0,1},{1,0},{2,3},{3,2},{4,5},{5,4},{6,7},{7,6},{8,9},{9,8},{10,11... | collective-permute-start | bytes 1179656 | tf_op jit(solution)/shard_map/ppermute | solution.py:620
  (8 other events, 80.5 us)
where the time goes:
time: 146 us; the launch traced here: 147 us
  Pallas kernels  80.8 us (55%)
  waiting for transfers between devices  29.3 us (20%)
  starting transfers between devices  28.4 us (19%)
  other arithmetic  5.36 us (4%)
  local copies, waits for them, and re-layouts  2.33 us (2%)
    pallas_call x3, Pallas kernels, attention(): pl.pallas_call(functools.partial(attention_kernel, clips, share, start, k...  27.3 us
    ppermute x3, waiting for transfers between devices, swap_tp(): return lax.ppermute(array, 'tp', [(0, 1), (1, 0)])  21.8 us
    pallas_call x4, Pallas kernels, project(): pl.pallas_call(functools.partial(project_kernel, ways, first, side, block...  17 us
    pallas_call x1, Pallas kernels, mlp_in(): pl.pallas_call(functools.partial(mlp_in_kernel, clips, len(parts)), grid=...  16.9 us
    ppermute x12, starting transfers between devices, exchange(): return lax.ppermute(array, 'ctx', pairs)  15.9 us
    pallas_call x1, Pallas kernels, mlp_out(): pl.pallas_call(mlp_out_kernel, grid=(width // block,), out_shape=jax.Shap...  11.8 us
    ppermute x7, starting transfers between devices, swap_cores(): return lax.ppermute(array, 'ctx', pairs)  6.88 us
    ppermute x3, starting transfers between devices, swap_tp(): return lax.ppermute(array, 'tp', [(0, 1), (1, 0)])  5.64 us
  transfers between devices with their start and end apart: 22, of which 10 were waited for; matrix products, arithmetic and copies ran while one was open for 3% of the time, Pallas kernels for 39%

commit v1 on v0

--- a/solution.py
+++ b/solution.py
@@ -10,7 +10,7 @@
 
 HD = 128
 LANES = 128
-ONES_ROWS = 8
+ONES_ROWS = 16
 KEY_WIDTH = 2 * HD
 MASKED = -3e38
 COST_SCALE = 1

time: 146 us -> 147 us (level)
  transfers between devices with their start and end apart: 22 -> 22, of which waited for: 10 -> 9; matrix products, arithmetic and copies ran while one was open for 3% -> 3% of each run, Pallas kernels for 39% -> 39%
where the time goes in v1:
time: 147 us
  Pallas kernels  80.5 us (55%)
  waiting for transfers between devices  30.7 us (21%)
  starting transfers between devices  28.1 us (19%)
  other arithmetic  5.36 us (4%)
  local copies, waits for them, and re-layouts  2.33 us (2%)
    pallas_call x3, Pallas kernels, attention(): pl.pallas_call(functools.partial(attention_kernel, clips, share, start, k...  27.1 us
    ppermute x3, waiting for transfers between devices, swap_tp(): return lax.ppermute(array, 'tp', [(0, 1), (1, 0)])  21.8 us
    pallas_call x4, Pallas kernels, project(): pl.pallas_call(functools.partial(project_kernel, ways, first, side, block...  17 us
    pallas_call x1, Pallas kernels, mlp_in(): pl.pallas_call(functools.partial(mlp_in_kernel, clips, len(parts)), grid=...  16.9 us
    ppermute x12, starting transfers between devices, exchange(): return lax.ppermute(array, 'ctx', pairs)  15.9 us
    pallas_call x1, Pallas kernels, mlp_out(): pl.pallas_call(mlp_out_kernel, grid=(width // block,), out_shape=jax.Shap...  11.8 us
    ppermute x7, starting transfers between devices, swap_cores(): return lax.ppermute(array, 'ctx', pairs)  6.88 us
    ppermute x3, starting transfers between devices, swap_tp(): return lax.ppermute(array, 'tp', [(0, 1), (1, 0)])  5.32 us
  transfers between devices with their start and end apart: 22, of which 9 were waited for; matrix products, arithmetic and copies ran while one was open for 3% of the time, Pallas kernels for 39%

profile of v1, /device:TPU:0, one launch (start us, length us, event | category | flops | bytes accessed | tf_op | source)
XLA Modules:
  0.0 147.3 jit_solution(16032195291163839359)
XLA Ops:
  0.6 4.3 %split_heads.1 = (bf16[4,3,384,128]{3,2,1,0:T(8,128)(2,1)}, bf16[4,3,384,128]{3,2,1,0:T(8,128)(2,1)}) custom-call(s32[3]{0:T(128)} %pad_add_fusion.1.place, bf16[384,1024]{1,0:T(8,128)(2,1)} %q_hbm.1, bf16[384,1024]{1,0:T(8,128)(2,1)} %k_hbm.1, bf16[384,1024]{1,0:T(8,128)(2,1)} %v_hbm.1), custom_call_target="tpu_custom_call" | custom-call | tf_op jit(solution)/shard_map/split_heads/pallas_call | solution.py:85
  5.4 2.6 %collective-permute-start = (bf16[384,1536]{1,0:T(8,128)(2,1)S(1)}, bf16[384,1536]{1,0:T(8,128)(2,1)S(1)}, u32[]{:S(2)}, u32[]{:S(2)}) collective-permute-start(bf16[384,1536]{1,0:T(8,128)(2,1)S(1)} %copy-done.2), channel_id=1, source_target_pairs={{0,1},{1,0},{2,3},{3,2},{4,5},{5,4},{6,7},{7,6},{8,9},{9,8},{10,11... | collective-permute-start | bytes 3538952 | tf_op jit(solution)/shard_map/ppermute | solution.py:620
  10.4 4.2 %collective-permute-start.5 = (bf16[3,2,384,128]{3,2,1,0:T(8,128)(2,1)S(1)}, bf16[3,2,384,128]{3,2,1,0:T(8,128)(2,1)S(1)}, u32[]{:S(2)}, u32[]{:S(2)}) collective-permute-start(bf16[3,2,384,128]{3,2,1,0:T(8,128)(2,1)S(1)} %get-tuple-element.68), channel_id=1, source_target_pairs={{0,24},{2,30},{4,28},{6,26},{8,16},{10,22},{12,20},{14,18},{16,8},... | collective-permute-start | bytes 1769480 | tf_op jit(solution)/shard_map/ppermute | solution.py:628
  16.0 18.5 %collective-permute-done.refs_1_ = bf16[384,1536]{1,0:T(8,128)(2,1)S(1)} collective-permute-done((bf16[384,1536]{1,0:T(8,128)(2,1)S(1)}, bf16[384,1536]{1,0:T(8,128)(2,1)S(1)}, u32[]{:S(2)}, u32[]{:S(2)}) %collective-permute-start) | collective-permute-done | bytes 1179680 | tf_op jit(solution)/shard_map/ppermute | solution.py:620
  34.5 16.9 %mlp_in.1.hidden = bf16[384,3072]{1,0:T(8,128)(2,1)S(1)} custom-call(s32[3]{0:T(128)S(1)} %copy-done.6, s32[384,1]{1,0:T(8,128)S(1)} %broadcast_in_dim.67.ids_ref, f32[3,4,3072]{2,1,0:T(4,128)S(1)} %copy-done.7, bf16[384,1536]{1,0:T(8,128)(2,1)S(1)} %copy-done.2, bf16[384,1536]{1,0:T(8,128)(2,1)S(1)} %collective-permute-done.refs_1_, bf16[3072,3072]{1,0:T(8,128)(2,1)} %refs_2_.1), custom_call_target="tpu_custom_call" | custom-call | flops 7247757312 | bytes 18874368 | tf_op jit(solution)/shard_map/mlp_in/pallas_call | solution.py:446
  51.5 11.8 %mlp_out.1.refs_6_ = f32[384,3072]{1,0:T(8,128)S(1)} custom-call(bf16[384,3072]{1,0:T(8,128)(2,1)S(1)} %mlp_in.1.hidden, bf16[3072,3072]{1,0:T(8,128)(2,1)} %w_out.1), custom_call_target="tpu_custom_call" | custom-call | flops 7247757312 | bytes 23592960 | tf_op jit(solution)/shard_map/mlp_out/pallas_call | solution.py:469
  63.3 2.7 %collective-permute-done.4.refs_2_.refs_0_ = bf16[3,2,384,128]{3,2,1,0:T(8,128)(2,1)S(1)} collective-permute-done((bf16[3,2,384,128]{3,2,1,0:T(8,128)(2,1)S(1)}, bf16[3,2,384,128]{3,2,1,0:T(8,128)(2,1)S(1)}, u32[]{:S(2)}, u32[]{:S(2)}) %collective-permute-start.4) | collective-permute-done | bytes 589856 | tf_op jit(solution)/shard_map/ppermute | solution.py:628
  70.6 2.6 %assemble.1 = (bf16[6144,256]{1,0:T(8,128)(2,1)S(1)}, bf16[144,6144]{1,0:T(8,128)(2,1)S(1)}) custom-call(s32[9]{0:T(128)S(1)} %pad_add_fusion.scalars, s32[3]{0:T(128)S(1)} %copy-done.6, bf16[3,2,384,128]{3,2,1,0:T(8,128)(2,1)S(1)} %collective-permute-done.2.refs_0_, bf16[3,2,384,128]{3,2,1,0:T(8,128)(2,1)S(1)} %collective-permute-done.3.refs_1_, ...), custom_call_target="tpu_custom_call" | custom-call | tf_op jit(solution)/shard_map/assemble/pallas_call | solution.py:192
  73.3 15.1 %attention_0.1 = (bf16[2,256,128]{2,1,0:T(8,128)(2,1)S(1)}, bf16[2,256,128]{2,1,0:T(8,128)(2,1)S(1)}, bf16[2,256,128]{2,1,0:T(8,128)(2,1)S(1)}, bf16[2,256,128]{2,1,0:T(8,128)(2,1)S(1)}) custom-call(s32[9]{0:T(128)S(1)} %pad_add_fusion.scalars, s32[3]{0:T(128)S(1)} %copy-done.6, bf16[6144,256]{1,0:T(8,128)(2,1)S(1)} %get-tuple-element.76.k, ...), custom_call_target="tpu_custom_call" | custom-call | flops 6442450944 | bytes 3145728 | tf_op jit(solution)/shard_map/attention_0/pallas_call | solution.py:375
  89.3 3.0 %collective-permute-start.12 = (bf16[2,256,128]{2,1,0:T(8,128)(2,1)S(1)}, bf16[2,256,128]{2,1,0:T(8,128)(2,1)S(1)}, u32[]{:S(2)}, u32[]{:S(2)}) collective-permute-start(bf16[2,256,128]{2,1,0:T(8,128)(2,1)S(1)} %get-tuple-element.80), channel_id=1, source_target_pairs={{0,16},{2,22},{4,20},{6,18},{8,24},{10,30},{12,28},{14,26},{16,0},... | collective-permute-start | bytes 393224 | tf_op jit(solution)/shard_map/ppermute | solution.py:628
  93.7 5.3 %attention_1_far.1 = (bf16[2,128,128]{2,1,0:T(8,128)(2,1)S(1)}, bf16[2,128,128]{2,1,0:T(8,128)(2,1)S(1)}) custom-call(s32[9]{0:T(128)S(1)} %pad_add_fusion.scalars, s32[3]{0:T(128)S(1)} %copy-done.6, bf16[6144,256]{1,0:T(8,128)(2,1)S(1)} %get-tuple-element.76.k, bf16[144,6144]{1,0:T(8,128)(2,1)S(1)} %get-tuple-element.77.v, ...), custom_call_target="tpu_custom_call" | custom-call | flops 1610612736 | bytes 3145728 | tf_op jit(solution)/shard_map/attention_1_far/pallas_call | solution.py:375
  99.1 1.9 %collective-permute-done.13.refs_3_ = bf16[2,256,128]{2,1,0:T(8,128)(2,1)S(1)} collective-permute-done((bf16[2,256,128]{2,1,0:T(8,128)(2,1)S(1)}, bf16[2,256,128]{2,1,0:T(8,128)(2,1)S(1)}, u32[]{:S(2)}, u32[]{:S(2)}) %collective-permute-start.13) | collective-permute-done | bytes 131104 | tf_op jit(solution)/shard_map/ppermute | solution.py:628
  101.3 3.8 %collective-permute-start.16 = (bf16[4,256,128]{2,1,0:T(8,128)(2,1)S(1)}, bf16[4,256,128]{2,1,0:T(8,128)(2,1)S(1)}, u32[]{:S(2)}, u32[]{:S(2)}) collective-permute-start(bf16[4,256,128]{2,1,0:T(8,128)(2,1)S(1)} %pick_others.2), channel_id=1, source_target_pairs={{0,2},{2,0},{4,6},{6,4},{8,10},{10,8},{12,14},{14,12},{16,18},{18,... | collective-permute-start | bytes 786440 | tf_op jit(solution)/shard_map/ppermute | solution.py:624
  105.1 2.9 %collective-permute-start.14 = (bf16[2,128,128]{2,1,0:T(8,128)(2,1)S(1)}, bf16[2,128,128]{2,1,0:T(8,128)(2,1)S(1)}, u32[]{:S(2)}, u32[]{:S(2)}) collective-permute-start(bf16[2,128,128]{2,1,0:T(8,128)(2,1)S(1)} %get-tuple-element.85), channel_id=1, source_target_pairs={{0,16},{2,22},{4,20},{6,18},{8,24},{10,30},{12,28},{14,26},{16,0},... | collective-permute-start | bytes 196616 | tf_op jit(solution)/shard_map/ppermute | solution.py:628
  109.4 4.4 %project_sent_0.1 = bf16[128,3072]{1,0:T(8,128)(2,1)S(1)} custom-call(s32[3]{0:T(128)S(1)} %copy-done.6, bf16[2,256,128]{2,1,0:T(8,128)(2,1)S(1)} %collective-permute-done.10.refs_0_, bf16[2,256,128]{2,1,0:T(8,128)(2,1)S(1)} %collective-permute-done.11.refs_1_, bf16[2,256,128]{2,1,0:T(8,128)(2,1)S(1)} %collective-permute-done.12.refs_2_, ...), custom_call_target="tpu_custom_call" | custom-call | flops 1 | bytes 1 | tf_op jit(solution)/shard_map/project_sent_0/pallas_call | solution.py:519
  113.7 1.6 %collective-permute-start.20 = (bf16[128,3072]{1,0:T(8,128)(2,1)S(1)}, bf16[128,3072]{1,0:T(8,128)(2,1)}, u32[]{:S(2)}, u32[]{:S(2)}) collective-permute-start(bf16[128,3072]{1,0:T(8,128)(2,1)S(1)} %project_sent_0.1), channel_id=1, source_target_pairs={{0,1},{1,0},{2,3},{3,2},{4,5},{5,4},{6,7},{7,6},{8,9},{9,8},{10,11... | collective-permute-start | bytes 2359304 | tf_op jit(solution)/shard_map/ppermute | solution.py:620
  115.3 6.7 %attention_1_near.1 = (bf16[2,128,128]{2,1,0:T(8,128)(2,1)S(1)}, bf16[2,128,128]{2,1,0:T(8,128)(2,1)S(1)}) custom-call(s32[9]{0:T(128)S(1)} %pad_add_fusion.scalars, s32[3]{0:T(128)S(1)} %copy-done.6, bf16[6144,256]{1,0:T(8,128)(2,1)S(1)} %get-tuple-element.76.k, bf16[144,6144]{1,0:T(8,128)(2,1)S(1)} %get-tuple-element.77.v, ...), custom_call_target="tpu_custom_call" | custom-call | flops 1610612736 | bytes 3145728 | tf_op jit(solution)/shard_map/attention_1_near/pallas_call | solution.py:375
  122.8 4.4 %project_kept_0.1 = f32[128,3072]{1,0:T(8,128)S(1)} custom-call(s32[3]{0:T(128)S(1)} %copy-done.6, bf16[2,256,128]{2,1,0:T(8,128)(2,1)S(1)} %collective-permute-done.10.refs_0_, bf16[2,256,128]{2,1,0:T(8,128)(2,1)S(1)} %collective-permute-done.11.refs_1_, bf16[2,256,128]{2,1,0:T(8,128)(2,1)S(1)} %collective-permute-done.12.refs_2_, ...), custom_call_target="tpu_custom_call" | custom-call | flops 1 | bytes 1 | tf_op jit(solution)/shard_map/project_kept_0/pallas_call | solution.py:519
  127.4 1.6 %collective-permute-start.19 = (bf16[4,128,128]{2,1,0:T(8,128)(2,1)S(1)}, bf16[4,128,128]{2,1,0:T(8,128)(2,1)S(1)}, u32[]{:S(2)}, u32[]{:S(2)}) collective-permute-start(bf16[4,128,128]{2,1,0:T(8,128)(2,1)S(1)} %pick_others.3), channel_id=1, source_target_pairs={{0,2},{2,0},{4,6},{6,4},{8,10},{10,8},{12,14},{14,12},{16,18},{18,... | collective-permute-start | bytes 393224 | tf_op jit(solution)/shard_map/ppermute | solution.py:624
  130.0 4.1 %project_sent_1.1 = bf16[64,3072]{1,0:T(8,128)(2,1)S(1)} custom-call(s32[3]{0:T(128)S(1)} %copy-done.6, bf16[2,128,128]{2,1,0:T(8,128)(2,1)S(1)} %collective-permute-done.17.refs_0_, bf16[2,128,128]{2,1,0:T(8,128)(2,1)S(1)} %collective-permute-done.18.refs_1_, bf16[2,128,128]{2,1,0:T(8,128)(2,1)S(1)} %collective-permute-done.14.refs_2_, ...), custom_call_target="tpu_custom_call" | custom-call | flops 1 | bytes 1 | tf_op jit(solution)/shard_map/project_sent_1/pallas_call | solution.py:519
  136.5 1.5 %fusion = f32[128,3072]{1,0:T(8,128)S(1)} fusion(f32[192,3072]{1,0:T(8,128)S(1)} %select_select_fusion, f32[192,3072]{1,0:T(8,128)S(1)} %fusion.1, f32[128,3072]{1,0:T(8,128)S(1)} %project_kept_0.1, bf16[128,3072]{1,0:T(8,128)(2,1)} %collective-permute-done.20), kind=kLoop, calls=%fused_computation.3 | loop fusion | flops 1572864 | bytes 7077888 | tf_op jit(solution)/shard_map/add | solution.py:704
  138.0 4.1 %project_kept_1.1 = f32[64,3072]{1,0:T(8,128)S(1)} custom-call(s32[3]{0:T(128)S(1)} %copy-done.6, bf16[2,128,128]{2,1,0:T(8,128)(2,1)S(1)} %collective-permute-done.17.refs_0_, bf16[2,128,128]{2,1,0:T(8,128)(2,1)S(1)} %collective-permute-done.18.refs_1_, bf16[2,128,128]{2,1,0:T(8,128)(2,1)S(1)} %collective-permute-done.14.refs_2_, ...), custom_call_target="tpu_custom_call" | custom-call | flops 1 | bytes 1 | tf_op jit(solution)/shard_map/project_kept_1/pallas_call | solution.py:519
  142.3 3.3 %collective-permute-done.21 = bf16[64,3072]{1,0:T(8,128)(2,1)S(1)} collective-permute-done((bf16[64,3072]{1,0:T(8,128)(2,1)S(1)}, bf16[64,3072]{1,0:T(8,128)(2,1)S(1)}, u32[]{:S(2)}, u32[]{:S(2)}) %collective-permute-start.21) | collective-permute-done | bytes 393248 | tf_op jit(solution)/shard_map/ppermute | solution.py:620
  145.7 1.6 %pad_maximum_fusion = f32[192,3072]{1,0:T(8,128)} fusion(f32[64,3072]{1,0:T(8,128)S(1)} %multiply_add_fusion, f32[128,3072]{1,0:T(8,128)S(1)} %fusion), kind=kLoop, calls=%fused_computation | loop fusion | flops 589824 | bytes 4718592 | tf_op jit(solution)/shard_map/concatenate | solution.py:708
  (68 shorter events, 18.0 us)
Async XLA Ops:
  0.6 33.9 %copy-start.6 = (s32[3]{0:T(128)S(1)}, s32[3]{0:T(128)}, u32[]{:S(2)}) copy-start(s32[3]{0:T(128)} %pad_add_fusion.1.place) | copy-start | bytes 40
  4.9 4.0 %collective-permute-start.1 = (bf16[4,3,384,128]{3,2,1,0:T(8,128)(2,1)}, bf16[4,3,384,128]{3,2,1,0:T(8,128)(2,1)S(1)}, u32[]{:S(2)}, u32[]{:S(2)}) collective-permute-start(bf16[4,3,384,128]{3,2,1,0:T(8,128)(2,1)} %get-tuple-element.64), channel_id=1, source_target_pairs={{0,2},{2,0},{4,6},{6,4},{8,10},{10,8},{12,14},{14,12},{16,18},{18,... | collective-permute-start | bytes 3538952 | tf_op jit(solution)/shard_map/ppermute | solution.py:624
  5.4 29.1 %collective-permute-start = (bf16[384,1536]{1,0:T(8,128)(2,1)S(1)}, bf16[384,1536]{1,0:T(8,128)(2,1)S(1)}, u32[]{:S(2)}, u32[]{:S(2)}) collective-permute-start(bf16[384,1536]{1,0:T(8,128)(2,1)S(1)} %copy-done.2), channel_id=1, source_target_pairs={{0,1},{1,0},{2,3},{3,2},{4,5},{5,4},{6,7},{7,6},{8,9},{9,8},{10,11... | collective-permute-start | bytes 3538952 | tf_op jit(solution)/shard_map/ppermute | solution.py:620
  8.0 26.6 %copy-start.7 = (f32[3,4,3072]{2,1,0:T(4,128)S(1)}, f32[3,4,3072]{2,1,0:T(4,128)}, u32[]{:S(2)}) copy-start(f32[3,4,3072]{2,1,0:T(4,128)} %modulation_ref.1) | copy-start | bytes 442372
  10.4 52.9 %collective-permute-start.5 = (bf16[3,2,384,128]{3,2,1,0:T(8,128)(2,1)S(1)}, bf16[3,2,384,128]{3,2,1,0:T(8,128)(2,1)S(1)}, u32[]{:S(2)}, u32[]{:S(2)}) collective-permute-start(bf16[3,2,384,128]{3,2,1,0:T(8,128)(2,1)S(1)} %get-tuple-element.68), channel_id=1, source_target_pairs={{0,24},{2,30},{4,28},{6,26},{8,16},{10,22},{12,20},{14,18},{16,8},... | collective-permute-start | bytes 1769480 | tf_op jit(solution)/shard_map/ppermute | solution.py:628
  14.6 51.4 %collective-permute-start.4 = (bf16[3,2,384,128]{3,2,1,0:T(8,128)(2,1)S(1)}, bf16[3,2,384,128]{3,2,1,0:T(8,128)(2,1)S(1)}, u32[]{:S(2)}, u32[]{:S(2)}) collective-permute-start(bf16[3,2,384,128]{3,2,1,0:T(8,128)(2,1)S(1)} %get-tuple-element.67), channel_id=1, source_target_pairs={{0,16},{2,22},{4,20},{6,18},{8,24},{10,30},{12,28},{14,26},{16,0},... | collective-permute-start | bytes 1769480 | tf_op jit(solution)/shard_map/ppermute | solution.py:628
  14.6 51.4 %collective-permute-start.3 = (bf16[3,2,384,128]{3,2,1,0:T(8,128)(2,1)S(1)}, bf16[3,2,384,128]{3,2,1,0:T(8,128)(2,1)S(1)}, u32[]{:S(2)}, u32[]{:S(2)}) collective-permute-start(bf16[3,2,384,128]{3,2,1,0:T(8,128)(2,1)S(1)} %get-tuple-element.66), channel_id=1, source_target_pairs={{0,8},{2,14},{4,12},{6,10},{8,0},{10,6},{12,4},{14,2},{16,24},{18,... | collective-permute-start | bytes 1769480 | tf_op jit(solution)/shard_map/ppermute | solution.py:628
  15.3 50.8 %collective-permute-start.2 = (bf16[3,2,384,128]{3,2,1,0:T(8,128)(2,1)S(1)}, bf16[3,2,384,128]{3,2,1,0:T(8,128)(2,1)S(1)}, u32[]{:S(2)}, u32[]{:S(2)}) collective-permute-start(bf16[3,2,384,128]{3,2,1,0:T(8,128)(2,1)S(1)} %get-tuple-element.65), channel_id=1, source_target_pairs={{0,0},{2,6},{4,4},{6,2},{8,8},{10,14},{12,12},{14,10},{16,16},{18,... | collective-permute-start | bytes 1769480 | tf_op jit(solution)/shard_map/ppermute | solution.py:628
  66.1 2.0 %collective-permute-start.6 = (bf16[3,2,384,128]{3,2,1,0:T(8,128)(2,1)S(1)}, bf16[3,2,384,128]{3,2,1,0:T(8,128)(2,1)S(1)}, u32[]{:S(2)}, u32[]{:S(2)}) collective-permute-start(bf16[3,2,384,128]{3,2,1,0:T(8,128)(2,1)S(1)} %collective-permute-done.2.refs_0_), channel_id=1, source_target_pairs={{0,2},{2,0},{4,6},{6,4},{8,10},{10,8},{12,14},{14,12},{16,18},{18,... | collective-permute-start | bytes 1769480 | tf_op jit(solution)/shard_map/ppermute | solution.py:624
  66.1 2.8 %collective-permute-start.7 = (bf16[3,2,384,128]{3,2,1,0:T(8,128)(2,1)S(1)}, bf16[3,2,384,128]{3,2,1,0:T(8,128)(2,1)S(1)}, u32[]{:S(2)}, u32[]{:S(2)}) collective-permute-start(bf16[3,2,384,128]{3,2,1,0:T(8,128)(2,1)S(1)} %collective-permute-done.3.refs_1_), channel_id=1, source_target_pairs={{0,2},{2,0},{4,6},{6,4},{8,10},{10,8},{12,14},{14,12},{16,18},{18,... | collective-permute-start | bytes 1769480 | tf_op jit(solution)/shard_map/ppermute | solution.py:624
  66.6 3.2 %collective-permute-start.8 = (bf16[3,2,384,128]{3,2,1,0:T(8,128)(2,1)S(1)}, bf16[3,2,384,128]{3,2,1,0:T(8,128)(2,1)S(1)}, u32[]{:S(2)}, u32[]{:S(2)}) collective-permute-start(bf16[3,2,384,128]{3,2,1,0:T(8,128)(2,1)S(1)} %collective-permute-done.4.refs_2_.refs_0_), channel_id=1, source_target_pairs={{0,2},{2,0},{4,6},{6,4},{8,10},{10,8},{12,14},{14,12},{16,18},{18,... | collective-permute-start | bytes 1769480 | tf_op jit(solution)/shard_map/ppermute | solution.py:624
  66.6 4.0 %collective-permute-start.9 = (bf16[3,2,384,128]{3,2,1,0:T(8,128)(2,1)S(1)}, bf16[3,2,384,128]{3,2,1,0:T(8,128)(2,1)S(1)}, u32[]{:S(2)}, u32[]{:S(2)}) collective-permute-start(bf16[3,2,384,128]{3,2,1,0:T(8,128)(2,1)S(1)} %collective-permute-done.5.refs_3_.refs_1_), channel_id=1, source_target_pairs={{0,2},{2,0},{4,6},{6,4},{8,10},{10,8},{12,14},{14,12},{16,18},{18,... | collective-permute-start | bytes 1769480 | tf_op jit(solution)/shard_map/ppermute | solution.py:624
  88.4 10.6 %collective-permute-start.10 = (bf16[2,256,128]{2,1,0:T(8,128)(2,1)S(1)}, bf16[2,256,128]{2,1,0:T(8,128)(2,1)S(1)}, u32[]{:S(2)}, u32[]{:S(2)}) collective-permute-start(bf16[2,256,128]{2,1,0:T(8,128)(2,1)S(1)} %get-tuple-element.78), channel_id=1, source_target_pairs={{0,0},{2,6},{4,4},{6,2},{8,8},{10,14},{12,12},{14,10},{16,16},{18,... | collective-permute-start | bytes 393224 | tf_op jit(solution)/shard_map/ppermute | solution.py:628
  89.2 9.8 %collective-permute-start.11 = (bf16[2,256,128]{2,1,0:T(8,128)(2,1)S(1)}, bf16[2,256,128]{2,1,0:T(8,128)(2,1)S(1)}, u32[]{:S(2)}, u32[]{:S(2)}) collective-permute-start(bf16[2,256,128]{2,1,0:T(8,128)(2,1)S(1)} %get-tuple-element.79), channel_id=1, source_target_pairs={{0,8},{2,14},{4,12},{6,10},{8,0},{10,6},{12,4},{14,2},{16,24},{18,... | collective-permute-start | bytes 393224 | tf_op jit(solution)/shard_map/ppermute | solution.py:628
  89.3 9.7 %collective-permute-start.12 = (bf16[2,256,128]{2,1,0:T(8,128)(2,1)S(1)}, bf16[2,256,128]{2,1,0:T(8,128)(2,1)S(1)}, u32[]{:S(2)}, u32[]{:S(2)}) collective-permute-start(bf16[2,256,128]{2,1,0:T(8,128)(2,1)S(1)} %get-tuple-element.80), channel_id=1, source_target_pairs={{0,16},{2,22},{4,20},{6,18},{8,24},{10,30},{12,28},{14,26},{16,0},... | collective-permute-start | bytes 393224 | tf_op jit(solution)/shard_map/ppermute | solution.py:628
  92.3 8.6 %collective-permute-start.13 = (bf16[2,256,128]{2,1,0:T(8,128)(2,1)S(1)}, bf16[2,256,128]{2,1,0:T(8,128)(2,1)S(1)}, u32[]{:S(2)}, u32[]{:S(2)}) collective-permute-start(bf16[2,256,128]{2,1,0:T(8,128)(2,1)S(1)} %get-tuple-element.81), channel_id=1, source_target_pairs={{0,24},{2,30},{4,28},{6,26},{8,16},{10,22},{12,20},{14,18},{16,8},... | collective-permute-start | bytes 393224 | tf_op jit(solution)/shard_map/ppermute | solution.py:628
  101.3 8.1 %collective-permute-start.16 = (bf16[4,256,128]{2,1,0:T(8,128)(2,1)S(1)}, bf16[4,256,128]{2,1,0:T(8,128)(2,1)S(1)}, u32[]{:S(2)}, u32[]{:S(2)}) collective-permute-start(bf16[4,256,128]{2,1,0:T(8,128)(2,1)S(1)} %pick_others.2), channel_id=1, source_target_pairs={{0,2},{2,0},{4,6},{6,4},{8,10},{10,8},{12,14},{14,12},{16,18},{18,... | collective-permute-start | bytes 786440 | tf_op jit(solution)/shard_map/ppermute | solution.py:624
  105.1 16.9 %collective-permute-start.14 = (bf16[2,128,128]{2,1,0:T(8,128)(2,1)S(1)}, bf16[2,128,128]{2,1,0:T(8,128)(2,1)S(1)}, u32[]{:S(2)}, u32[]{:S(2)}) collective-permute-start(bf16[2,128,128]{2,1,0:T(8,128)(2,1)S(1)} %get-tuple-element.85), channel_id=1, source_target_pairs={{0,16},{2,22},{4,20},{6,18},{8,24},{10,30},{12,28},{14,26},{16,0},... | collective-permute-start | bytes 196616 | tf_op jit(solution)/shard_map/ppermute | solution.py:628
  108.0 14.0 %collective-permute-start.15 = (bf16[2,128,128]{2,1,0:T(8,128)(2,1)S(1)}, bf16[2,128,128]{2,1,0:T(8,128)(2,1)S(1)}, u32[]{:S(2)}, u32[]{:S(2)}) collective-permute-start(bf16[2,128,128]{2,1,0:T(8,128)(2,1)S(1)} %get-tuple-element.86), channel_id=1, source_target_pairs={{0,24},{2,30},{4,28},{6,26},{8,16},{10,22},{12,20},{14,18},{16,8},... | collective-permute-start | bytes 196616 | tf_op jit(solution)/shard_map/ppermute | solution.py:628
  113.7 20.4 %collective-permute-start.20 = (bf16[128,3072]{1,0:T(8,128)(2,1)S(1)}, bf16[128,3072]{1,0:T(8,128)(2,1)}, u32[]{:S(2)}, u32[]{:S(2)}) collective-permute-start(bf16[128,3072]{1,0:T(8,128)(2,1)S(1)} %project_sent_0.1), channel_id=1, source_target_pairs={{0,1},{1,0},{2,3},{3,2},{4,5},{5,4},{6,7},{7,6},{8,9},{9,8},{10,11... | collective-permute-start | bytes 2359304 | tf_op jit(solution)/shard_map/ppermute | solution.py:620
  122.0 5.1 %collective-permute-start.17 = (bf16[2,128,128]{2,1,0:T(8,128)(2,1)S(1)}, bf16[2,128,128]{2,1,0:T(8,128)(2,1)S(1)}, u32[]{:S(2)}, u32[]{:S(2)}) collective-permute-start(bf16[2,128,128]{2,1,0:T(8,128)(2,1)S(1)} %get-tuple-element.95), channel_id=1, source_target_pairs={{0,0},{2,6},{4,4},{6,2},{8,8},{10,14},{12,12},{14,10},{16,16},{18,... | collective-permute-start | bytes 196616 | tf_op jit(solution)/shard_map/ppermute | solution.py:628
  122.7 4.5 %collective-permute-start.18 = (bf16[2,128,128]{2,1,0:T(8,128)(2,1)S(1)}, bf16[2,128,128]{2,1,0:T(8,128)(2,1)S(1)}, u32[]{:S(2)}, u32[]{:S(2)}) collective-permute-start(bf16[2,128,128]{2,1,0:T(8,128)(2,1)S(1)} %get-tuple-element.96), channel_id=1, source_target_pairs={{0,8},{2,14},{4,12},{6,10},{8,0},{10,6},{12,4},{14,2},{16,24},{18,... | collective-permute-start | bytes 196616 | tf_op jit(solution)/shard_map/ppermute | solution.py:628
  127.4 2.6 %collective-permute-start.19 = (bf16[4,128,128]{2,1,0:T(8,128)(2,1)S(1)}, bf16[4,128,128]{2,1,0:T(8,128)(2,1)S(1)}, u32[]{:S(2)}, u32[]{:S(2)}) collective-permute-start(bf16[4,128,128]{2,1,0:T(8,128)(2,1)S(1)} %pick_others.3), channel_id=1, source_target_pairs={{0,2},{2,0},{4,6},{6,4},{8,10},{10,8},{12,14},{14,12},{16,18},{18,... | collective-permute-start | bytes 393224 | tf_op jit(solution)/shard_map/ppermute | solution.py:624
  134.1 11.4 %collective-permute-start.21 = (bf16[64,3072]{1,0:T(8,128)(2,1)S(1)}, bf16[64,3072]{1,0:T(8,128)(2,1)S(1)}, u32[]{:S(2)}, u32[]{:S(2)}) collective-permute-start(bf16[64,3072]{1,0:T(8,128)(2,1)S(1)} %project_sent_1.1), channel_id=1, source_target_pairs={{0,1},{1,0},{2,3},{3,2},{4,5},{5,4},{6,7},{7,6},{8,9},{9,8},{10,11... | collective-permute-start | bytes 1179656 | tf_op jit(solution)/shard_map/ppermute | solution.py:620
  (8 other events, 77.6 us)
